TPU v7x, 128 devices: a whole 4x4x4 slice. The times are simulated.
128 devices in a mesh: grp: 8 (over y, core), leaf: 16 (over x, z).
Axes of the slice: x: 4, y: 4, z: 4, core: 2. Of those that a mesh axis runs over, the one named last changes fastest.
Arguments:
- points: bfloat16 [32, 262144], P(None, ('grp', 'leaf')), may hold values from -6 to 6
- right_side: float32 [8, 262144], P(None, ('grp', 'leaf')), may hold values from -6 to 6
- neighbours: int32 [256, 8], P(('grp', 'leaf')), may hold values from 0 to 31, as said below
- neighbour_count: int32 [256], P(('grp', 'leaf')), may hold values from 1 to 8, as said below
- mid_skeleton: int32 [128, 256], P(('grp', 'leaf')), may hold values from 0 to 2047, as said below
- top_skeleton: int32 [8, 256], P('grp'), may hold values from 0 to 32767, as said below
- mid_basis: float32 [256, 262144], P(None, ('grp', 'leaf')), may hold values from -0.125 to 0.125
- top_basis: float32 [256, 262144], P(None, ('grp', 'leaf')), may hold values from -0.125 to 0.125
- noise_level: float32 [1], replicated, may hold values from 1 to 2
Outputs:
- solution: float32 [8, 262144], P(None, ('grp', 'leaf'))
- residual: float32 [8, 262144], P(None, ('grp', 'leaf'))
Inputs may be any that keep to these rules, and one draw needn't show every extreme that they name: `neighbours`: entry 0 of leaf l is l itself; entries 1 to neighbour_count[l] - 1 are distinct other leaves of the same subtree; later entries repeat l. Leaf j is listed by l exactly when l is listed by j. `neighbour_count`: the number of listed entries of each leaf, itself included. `mid_skeleton`: distinct positions within each block. `top_skeleton`: distinct positions within each subtree.
All inputs are finite; a program needn't handle non-finite values.
Results may differ from a plain program's by a relative error of at most 0.0003.
Values may be sent and summed in bfloat16 or wider, within the bound.
A program may use at most 128 MiB of HBM per device.

v0:
```python
import math

import jax
import jax.numpy as jnp
from jax import lax
from jax.experimental import pallas as pl
from jax.experimental.pallas import tpu as pltpu
from jax.sharding import PartitionSpec as P

FEATURES = 32
TARGETS = 8
WIDE = FEATURES + 2 * TARGETS
LEAF = 1024
RANK = 256
SLOTS = 8
SIDE = 4
N_LEAF = 16
N_GRP = 8
BLOCK = 2 * LEAF
CHUNK = 512
KEPT = 11
MESH = pl.DeviceIdType.MESH
F32 = jnp.float32
BF16 = jnp.bfloat16
SCALE = math.log2(math.e) / 16.0

LABELS = [(1, 0), (3, 0), (2, 0)] + [(df, ds) for df in range(4) for ds in (1, 3, 2)]
PLACE = {label: i for i, label in enumerate(LABELS)}


def dot(left, right):
    return jnp.dot(left, right, preferred_element_type=F32)


def dot_tn(left, right):
    return lax.dot_general(left, right, (((0,), (0,)), ((), ())), preferred_element_type=F32)


def dot_nt(left, right):
    return lax.dot_general(left, right, (((1,), (1,)), ((), ())), preferred_element_type=F32)


def halves(value):
    high = value.astype(BF16)
    return high, (value - high.astype(F32)).astype(BF16)


def stacked(value):
    high = value.astype(BF16).astype(F32)
    return jnp.concatenate([high, value - high], axis=0).astype(BF16)


def folded(value):
    return value[:TARGETS] + value[TARGETS:]


def thirds(coords):
    scaled = coords.astype(F32) * SCALE
    first = scaled.astype(BF16)
    rest = scaled - first.astype(F32)
    second = rest.astype(BF16)
    third = (rest - second.astype(F32)).astype(BF16)
    return jnp.concatenate([first, second, third], axis=0)


def self_scale(coords):
    wide = coords.astype(F32)
    return jnp.exp2(jnp.sum(wide * wide, axis=0, keepdims=True) * (-0.5 * SCALE))


def kernel_halves(rows, columns3):
    return halves(jnp.exp2(dot_tn(jnp.concatenate([rows, rows, rows], axis=0), columns3)))


def applied(field16, high, low):
    return dot(field16, high) + dot(field16, low)


class Gather:
    def __init__(self, half, me, slot, send, recv):
        first, second = lax.div(me, SIDE), lax.rem(me, SIDE)
        if half == 1:
            first, second = second, first
        self.half, self.first, self.second = half, first, second
        self.slot, self.send, self.recv = slot, send, recv
        self.sent = []

    def device(self, df, ds):
        f = lax.rem(self.first + SIDE - df, SIDE)
        s = lax.rem(self.second + SIDE - ds, SIDE)
        return f * SIDE + s if self.half == 0 else s * SIDE + f

    def copy(self, mine, label, to):
        place = self.half * len(LABELS) + PLACE[label]
        ref = self.slot(self.device(*mine))
        return pltpu.make_async_remote_copy(
            src_ref=ref,
            dst_ref=ref,
            send_sem=self.send.at[place],
            recv_sem=self.recv.at[place],
            device_id={"leaf": to},
            device_id_type=MESH,
        )

    def push(self, mine, label, to):
        copy = self.copy(mine, label, to)
        copy.start()
        self.sent.append(copy)

    def wait(self, *labels):
        for label in labels:
            self.copy(label, label, self.device(1, 0)).wait_recv()

    def along_first(self, ahead):
        return self.device(3 if ahead else 1, 0)

    def along_second(self, ahead):
        return self.device(0, 3 if ahead else 1)

    def spread(self, df):
        self.push((df, 0), (df, 1), self.along_second(True))
        self.push((df, 0), (df, 3), self.along_second(False))

    def relay(self, df):
        came = (df, 1 if df % 2 == 0 else 3)
        self.wait(came)
        self.push(came, (df, 2), self.along_second(df % 2 == 0))

    def own(self):
        self.push((0, 0), (1, 0), self.along_first(True))
        self.push((0, 0), (3, 0), self.along_first(False))
        self.spread(0)

    def near(self):
        self.wait((1, 0))
        self.push((1, 0), (2, 0), self.along_first(True))
        self.spread(1)
        self.wait((3, 0))
        self.spread(3)
        self.relay(0)

    def far(self):
        self.wait((2, 0))
        self.spread(2)
        self.relay(1)
        self.relay(3)

    def last(self):
        self.relay(2)

    def arrive(self):
        self.wait((0, 3), (1, 1), (3, 1), (2, 3), (0, 2), (1, 2), (3, 2), (2, 2))

    def finish(self):
        for copy in self.sent:
            copy.wait_send()


class Exchange:
    def __init__(self, axis, size, me, block, send, recv):
        self.axis, self.size, self.me, self.block = axis, size, me, block
        self.send, self.recv = send, recv
        self.sent = []

    def copy(self, owner, step, to):
        ref = self.block(owner)
        return pltpu.make_async_remote_copy(
            src_ref=ref,
            dst_ref=ref,
            send_sem=self.send.at[step],
            recv_sem=self.recv.at[step],
            device_id={self.axis: to},
            device_id_type=MESH,
        )

    def start(self):
        for step in range(1, self.size):
            copy = self.copy(self.me, step, lax.rem(self.me + step, self.size))
            copy.start()
            self.sent.append(copy)

    def wait(self):
        for step in range(1, self.size):
            owner = lax.rem(self.me + self.size - step, self.size)
            self.copy(owner, step, owner).wait_recv()

    def finish(self):
        for copy in self.sent:
            copy.wait_send()


def body(
    points_ref,
    right_ref,
    listed_ref,
    count_ref,
    mid_pick_ref,
    top_pick_ref,
    mid_basis_ref,
    top_basis_ref,
    noise_ref,
    solution_ref,
    residual_ref,
    direction_ref,
    image_ref,
    step_ref,
    blocks,
    fields1,
    own3,
    smalls,
    roots,
    weights,
    tops,
    sums_leaf,
    sums_grp,
    basis,
    basis_high,
    basis_low,
    near_sum,
    image,
    term,
    kept,
    basis_sem,
    blocks_send,
    blocks_recv,
    smalls_send,
    smalls_recv,
    image0_send,
    image0_recv,
    image1_send,
    image1_recv,
    roots_send,
    roots_recv,
    weights_send,
    weights_recv,
    tops_send,
    tops_recv,
    sums_leaf_send,
    sums_leaf_recv,
    sums_grp_send,
    sums_grp_recv,
):
    me, grp = lax.axis_index("leaf"), lax.axis_index("grp")

    loads = [
        pltpu.make_async_copy(ref, basis.at[i], basis_sem.at[i])
        for i, ref in enumerate((mid_basis_ref, top_basis_ref))
    ]
    for load in loads:
        load.start()

    barrier = pltpu.get_barrier_semaphore()
    x, z = lax.div(me, SIDE), lax.rem(me, SIDE)
    beside = [{"leaf": lax.rem(x + step, SIDE) * SIDE + z} for step in (1, 3)]
    beside += [{"leaf": x * SIDE + lax.rem(z + step, SIDE)} for step in (1, 3)]
    beside += [{"grp": lax.rem(grp + step, N_GRP)} for step in range(1, N_GRP)]
    for device in beside:
        pl.semaphore_signal(barrier, inc=1, device_id=device, device_id_type=MESH)

    points = points_ref[...]
    right = right_ref[...]
    scale = self_scale(points)
    field = right * scale
    for slot in range(2):
        columns = slice(slot * LEAF, (slot + 1) * LEAF)
        blocks[2 * me + slot, 0:FEATURES] = points[:, columns]
        blocks[2 * me + slot, FEATURES:WIDE] = stacked(field[:, columns])
        own3[slot] = thirds(points[:, columns])

    pl.semaphore_wait(barrier, len(beside))

    def gathers(slot_of, send, recv):
        return [
            Gather(half, me, lambda dev, half=half: slot_of(half, dev), send, recv)
            for half in range(2)
        ]

    block_gathers = gathers(
        lambda half, dev: blocks.at[2 * dev + half], blocks_send, blocks_recv
    )
    small_gathers = gathers(lambda half, dev: smalls.at[half, dev], smalls_send, smalls_recv)
    image_gather = gathers(
        lambda half, dev: fields1.at[2 * dev + half], image0_send, image0_recv
    )[:1]
    image_exchange = Exchange(
        "leaf", N_LEAF, me, lambda dev: fields1.at[2 * dev + 1], image1_send, image1_recv
    )
    root_exchange = Exchange("grp", N_GRP, grp, lambda g: roots.at[g], roots_send, roots_recv)
    weight_exchange = Exchange(
        "leaf", N_LEAF, me, lambda dev: weights.at[dev], weights_send, weights_recv
    )
    top_exchange = Exchange("grp", N_GRP, grp, lambda g: tops.at[g], tops_send, tops_recv)
    leaf_exchange = Exchange(
        "leaf", N_LEAF, me, lambda dev: sums_leaf.at[dev], sums_leaf_send, sums_leaf_recv
    )
    grp_exchange = Exchange(
        "grp", N_GRP, grp, lambda g: sums_grp.at[g], sums_grp_send, sums_grp_recv
    )

    def step(gathered, *names):
        for name in names:
            for gather in gathered:
                getattr(gather, name)()

    def field_of(it, leaf):
        return blocks[leaf, FEATURES:WIDE, :] if it == 0 else fields1[leaf]

    def add_block(it, slot, place, rows_of, field16, weight):
        total = None
        for first in range(0, LEAF, CHUNK):
            rows = pl.ds(first, CHUNK)
            if it == 1 and place is not None:
                high, low = kept[place, 0, rows, :], kept[place, 1, rows, :]
            else:
                high, low = kernel_halves(rows_of(rows), own3[slot])
                if place is not None:
                    kept[place, 0, rows, :] = high
                    kept[place, 1, rows, :] = low
            part = applied(field16[:, first : first + CHUNK], high, low)
            total = part if total is None else total + part
        near_sum[slot] += total * weight

    def near_self(it, slot):
        near_sum[slot] = jnp.zeros((2 * TARGETS, LEAF), F32)
        base = slot * LEAF
        rows_of = lambda rows: points_ref[:, pl.ds(base + rows.start, rows.size)]
        field16 = field_of(it, 2 * me + slot)
        add_block(it, slot, None, rows_of, field16, count_ref[slot].astype(F32))

    def near_listed(it, slot, begin=1, end=SLOTS):
        count = count_ref[slot]

        def run(low_end, high_end, keep):
            def one(k, carried):
                leaf = listed_ref[slot, k]
                active = jnp.where(k < count, 1.0, 0.0).astype(F32)
                place = slot * (SLOTS - 1) + k - 1 if keep else None
                rows_of = lambda rows: blocks[leaf, 0:FEATURES, rows]
                add_block(it, slot, place, rows_of, field_of(it, leaf), active)
                return carried

            if low_end < high_end:
                lax.fori_loop(low_end, high_end, one, 0, unroll=True)

        limit = min(max(KEPT - slot * (SLOTS - 1) + 1, 1), SLOTS)
        run(begin, min(end, limit), True)
        run(max(begin, limit), end, False)

    def near(slot):
        return folded(near_sum[slot]) * (scale[:, slot * LEAF : (slot + 1) * LEAF] * LEAF**-0.5)

    def project(value):
        value16 = stacked(value)
        return folded(dot_nt(value16, basis_high[...]) + dot_nt(value16, basis_low[...]))

    def side_by_side(blocks):
        return jnp.concatenate(blocks, axis=1)

    def skeleton_image(coords_of, fields_of, count, columns3):
        total = jnp.zeros((2 * TARGETS, RANK), F32)
        for start in range(0, count, 4):
            rows = side_by_side([coords_of(start + i) for i in range(4)])
            field16 = side_by_side([fields_of(start + i) for i in range(4)])
            total = total + applied(field16, *kernel_halves(rows, columns3))
        return folded(total)

    step(block_gathers, "own")

    def picked(pick, base):
        found = jnp.zeros((FEATURES, RANK), F32)
        for start in range(0, BLOCK, CHUNK):
            rows = lax.broadcasted_iota(jnp.int32, (CHUNK, RANK), 0) + (base + start)
            chosen = jnp.where(rows == pick, 1.0, 0.0).astype(BF16)
            found = found + dot(points[:, start : start + CHUNK], chosen)
        return found.astype(BF16)

    own_mid = picked(mid_pick_ref[...], 0)
    mid3, mid_scale = thirds(own_mid), self_scale(own_mid)
    smalls[0, me, 0:FEATURES] = own_mid
    smalls[1, me, 0:FEATURES] = picked(top_pick_ref[...], me * BLOCK)

    for load in loads:
        load.wait()
    for i in range(2):
        for start in range(0, RANK, 64):
            high, low = halves(basis[i, start : start + 64, :])
            basis_high[i * RANK + start : i * RANK + start + 64, :] = high
            basis_low[i * RANK + start : i * RANK + start + 64, :] = low
    parts = project(right)
    smalls[0, me, FEATURES:WIDE] = stacked(parts[:, :RANK] * mid_scale)
    smalls[1, me, FEATURES:WIDE] = stacked(parts[:, RANK:])

    step(block_gathers, "near")
    step(small_gathers, "own")
    near_self(0, 0)
    step(block_gathers, "far")
    step(small_gathers, "near")
    near_self(0, 1)
    step(block_gathers, "last")
    step(small_gathers, "far")
    step(block_gathers, "arrive")

    def mid_image(fields_of):
        found = skeleton_image(
            lambda dev: smalls[0, dev, 0:FEATURES, :], fields_of, N_LEAF, mid3
        )
        return found * (mid_scale * RANK**-0.5)

    def expand(mid_part, fields_of):
        found = skeleton_image(
            lambda g: roots[g, 0:FEATURES, :], fields_of, N_GRP, root3
        )
        top_part = found * (root_scale * RANK**-0.5)
        image16 = stacked(side_by_side([mid_part, top_part]))
        for start in range(0, BLOCK, CHUNK):
            columns = slice(start, start + CHUNK)
            term[:, columns] = folded(
                applied(image16, basis_high[:, columns], basis_low[:, columns])
            )

    noise = noise_ref[0]

    def finished(value, slot):
        columns = slice(slot * LEAF, (slot + 1) * LEAF)
        return noise * value[:, columns] + near(slot) + term[:, columns]

    near_listed(0, 0, 1, 3)
    step(small_gathers, "last", "arrive")
    own_root, top = jnp.zeros((FEATURES, RANK), F32), jnp.zeros((2 * TARGETS, RANK), F32)
    for dev in range(N_LEAF):
        own_root = own_root + smalls[1, dev, 0:FEATURES, :].astype(F32)
        top = top + smalls[1, dev, FEATURES:WIDE, :].astype(F32)
    own_root = own_root.astype(BF16)
    root3, root_scale = thirds(own_root), self_scale(own_root)
    roots[grp, 0:FEATURES] = own_root
    roots[grp, FEATURES:WIDE] = stacked(folded(top) * root_scale)
    root_exchange.start()
    mid_part = mid_image(lambda dev: smalls[0, dev, FEATURES:WIDE, :])
    near_listed(0, 0, 3, SLOTS)
    root_exchange.wait()
    expand(mid_part, lambda g: roots[g, FEATURES:WIDE, :])

    def finish_image(slot):
        columns = slice(slot * LEAF, (slot + 1) * LEAF)
        found = finished(right, slot)
        image[:, columns] = found
        fields1[2 * me + slot] = stacked(found * scale[:, columns])

    finish_image(0)
    step(image_gather, "own")
    near_listed(0, 1, 1, 4)
    step(image_gather, "near")
    near_listed(0, 1, 4, 7)
    step(image_gather, "far")
    near_listed(0, 1, 7, SLOTS)
    finish_image(1)
    image_exchange.start()

    def summed(value):
        return jnp.sum(value, axis=1, keepdims=True)

    first_image = image[...]
    parts = project(first_image)
    lane = lax.broadcasted_iota(jnp.int32, (TARGETS, RANK), 1)
    weights[me, 0:8] = parts[:, :RANK] * mid_scale
    weights[me, 8:16] = parts[:, RANK:]
    weights[me, 16:24] = jnp.where(
        lane == 0,
        summed(right * right),
        jnp.where(lane == 1, summed(right * first_image), summed(first_image * first_image)),
    )
    weight_exchange.start()
    near_self(1, 0)
    step(image_gather, "last")
    near_self(1, 1)
    step(image_gather, "arrive")
    image_exchange.wait()
    near_listed(1, 0)
    weight_exchange.wait()
    sums = weights[0, 8:24]
    for dev in range(1, N_LEAF):
        sums = sums + weights[dev, 8:24]
    tops[grp, 0:8] = sums[0:8] * root_scale
    tops[grp, 8:16] = sums[8:16]
    top_exchange.start()
    mid_part = mid_image(lambda dev: stacked(weights[dev, 0:8]))
    near_listed(1, 1)
    top_exchange.wait()
    expand(mid_part, lambda g: stacked(tops[g, 0:8]))

    totals = tops[0, 8:16]
    for g in range(1, N_GRP):
        totals = totals + tops[g, 8:16]
    norm0, curve0, square0 = totals[:, 0:1], totals[:, 1:2], totals[:, 2:3]
    alpha = norm0 / curve0
    norm1 = norm0 - 2.0 * alpha * curve0 + alpha * alpha * square0
    beta = norm1 / norm0
    second_image = jnp.concatenate(
        [finished(first_image, slot) for slot in range(2)], axis=1
    )
    residual = right - alpha * first_image
    direction = residual + beta * right
    image1 = (1.0 + beta) * first_image - alpha * second_image
    solution_ref[...] = alpha * right
    residual_ref[...] = residual
    direction_ref[...] = direction
    image_ref[...] = image1

    diagonal = lax.broadcasted_iota(jnp.int32, (TARGETS, 128), 0) == lax.broadcasted_iota(
        jnp.int32, (TARGETS, 128), 1
    )
    curve1 = jnp.where(diagonal, summed(direction * image1), 0.0)
    sums_leaf[me] = jnp.sum(curve1, axis=0, keepdims=True)
    leaf_exchange.start()
    leaf_exchange.wait()
    total = sums_leaf[0]
    for dev in range(1, N_LEAF):
        total = total + sums_leaf[dev]
    sums_grp[grp] = total
    grp_exchange.start()
    grp_exchange.wait()
    total = sums_grp[0]
    for g in range(1, N_GRP):
        total = total + sums_grp[g]
    curve1 = summed(jnp.where(diagonal, total, 0.0))
    step_ref[...] = jnp.broadcast_to(norm1 / curve1, (TARGETS, BLOCK))

    for sender in (
        *block_gathers,
        *small_gathers,
        *image_gather,
        image_exchange,
        root_exchange,
        weight_exchange,
        top_exchange,
        leaf_exchange,
        grp_exchange,
    ):
        sender.finish()


def on_device(*operands):
    vmem, smem, anywhere = (
        pl.BlockSpec(memory_space=space) for space in (pltpu.VMEM, pltpu.SMEM, pl.ANY)
    )
    messages = 2 * len(LABELS)
    dma = pltpu.SemaphoreType.DMA
    out = jax.ShapeDtypeStruct((TARGETS, BLOCK), F32)
    solution1, residual1, direction, image1, step = pl.pallas_call(
        body,
        out_shape=(out,) * 5,
        in_specs=[vmem, vmem, smem, smem, vmem, vmem, anywhere, anywhere, smem],
        out_specs=(vmem,) * 5,
        scratch_shapes=[
            pltpu.VMEM((2 * N_LEAF, WIDE, LEAF), BF16),
            pltpu.VMEM((2 * N_LEAF, 2 * TARGETS, LEAF), BF16),
            pltpu.VMEM((2, 3 * FEATURES, LEAF), BF16),
            pltpu.VMEM((2, N_LEAF, WIDE, RANK), BF16),
            pltpu.VMEM((N_GRP, WIDE, RANK), BF16),
            pltpu.VMEM((N_LEAF, 3 * TARGETS, RANK), F32),
            pltpu.VMEM((N_GRP, 2 * TARGETS, RANK), F32),
            pltpu.VMEM((N_LEAF, 1, 128), F32),
            pltpu.VMEM((N_GRP, 1, 128), F32),
            pltpu.VMEM((2, RANK, BLOCK), F32),
            pltpu.VMEM((2 * RANK, BLOCK), BF16),
            pltpu.VMEM((2 * RANK, BLOCK), BF16),
            pltpu.VMEM((2, 2 * TARGETS, LEAF), F32),
            pltpu.VMEM((TARGETS, BLOCK), F32),
            pltpu.VMEM((TARGETS, BLOCK), F32),
            pltpu.VMEM((KEPT, 2, LEAF, LEAF), BF16),
            dma((2,)),
            dma((messages,)),
            dma((messages,)),
            dma((messages,)),
            dma((messages,)),
            dma((messages,)),
            dma((messages,)),
            dma((N_LEAF,)),
            dma((N_LEAF,)),
            dma((N_GRP,)),
            dma((N_GRP,)),
            dma((N_LEAF,)),
            dma((N_LEAF,)),
            dma((N_GRP,)),
            dma((N_GRP,)),
            dma((N_LEAF,)),
            dma((N_LEAF,)),
            dma((N_GRP,)),
            dma((N_GRP,)),
        ],
        compiler_params=pltpu.CompilerParams(
            collective_id=0, has_side_effects=True, vmem_limit_bytes=62 * 2**20
        ),
    )(*operands)
    return solution1 + step * direction, residual1 - step * image1


def solution(mesh):
    placed = (
        P(None, ("grp", "leaf")),
        P(None, ("grp", "leaf")),
        P(("grp", "leaf"), None),
        P(("grp", "leaf")),
        P(("grp", "leaf"), None),
        P("grp", None),
        P(None, ("grp", "leaf")),
        P(None, ("grp", "leaf")),
        P(),
    )
    return jax.shard_map(
        on_device,
        mesh=mesh,
        in_specs=placed,
        out_specs=(P(None, ("grp", "leaf")), P(None, ("grp", "leaf"))),
        check_vma=False,
    )
```

profile of v0, /device:TPU:1, one launch (start us, length us, event | category | flops | bytes accessed | tf_op | source)
XLA Modules:
  0.0 94.2 jit_solution(2684744548163200457)
XLA Ops:
  1.3 91.3 %shard_map.104 = (f32[8,2048]{1,0:T(8,128)}, f32[8,2048]{1,0:T(8,128)}, f32[8,2048]{1,0:T(8,128)}, f32[8,2048]{1,0:T(8,128)}, f32[8,2048]{1,0:T(8,128)}) custom-call(bf16[32,2048]{1,0:T(8,128)(2,1)} %points_ref.1, f32[8,2048]{1,0:T(8,128)} %right_ref.1, s32[2,8]{1,0:T(2,128)} %listed_ref.1, s32[2]{0:T(128)} %count_ref.1, s32[1,256]{1,0:T(1,128)} %mid_pick_ref.1, ...), custom_call_target="tpu_custom_call" | custom-call | tf_op jit(solution)/shard_map/pallas_call | solution.py:549
  92.6 1.6 %multiply_subtract_fusion = (f32[8,2048]{1,0:T(8,128)}, f32[8,2048]{1,0:T(8,128)}) fusion(f32[8,2048]{1,0:T(8,128)} %get-tuple-element.10, f32[8,2048]{1,0:T(8,128)} %get-tuple-element.8, f32[8,2048]{1,0:T(8,128)} %get-tuple-element.11, f32[8,2048]{1,0:T(8,128)} %get-tuple-element.7, f32[8,2048]{1,0:T(8,128)} %get-tuple-element.9), kind=kLoop, calls=%fused_computation | loop fusion | flops 65536 | bytes 458752 | tf_op jit(solution)/shard_map/sub | solution.py:595
where the time goes:
time: 94.4 us; the launch traced here: 94.2 us
  Pallas kernels  91.3 us (97%)
  other arithmetic  1.63 us (2%)
  between operations  1.29 us (1%)
    pallas_call x1, Pallas kernels, on_device(): pl.pallas_call(body, out_shape=(out,) * 5, in_specs=[vmem, vmem, smem, sm...  91.3 us

commit v1 on v0

--- a/solution.py
+++ b/solution.py
@@ -77,12 +77,12 @@
 
 
 class Gather:
-    def __init__(self, half, me, slot, send, recv):
+    def __init__(self, half, me, slot, send, recv, turn=0):
         first, second = lax.div(me, SIDE), lax.rem(me, SIDE)
         if half == 1:
             first, second = second, first
         self.half, self.first, self.second = half, first, second
-        self.slot, self.send, self.recv = slot, send, recv
+        self.slot, self.send, self.recv, self.turn = slot, send, recv, turn
         self.sent = []
 
     def device(self, df, ds):
@@ -121,10 +121,13 @@
         self.push((df, 0), (df, 1), self.along_second(True))
         self.push((df, 0), (df, 3), self.along_second(False))
 
+    def ahead(self, df):
+        return (df + self.turn) % 2 == 0
+
     def relay(self, df):
-        came = (df, 1 if df % 2 == 0 else 3)
+        came = (df, 1 if self.ahead(df) else 3)
         self.wait(came)
-        self.push(came, (df, 2), self.along_second(df % 2 == 0))
+        self.push(came, (df, 2), self.along_second(self.ahead(df)))
 
     def own(self):
         self.push((0, 0), (1, 0), self.along_first(True))
@@ -132,11 +135,12 @@
         self.spread(0)
 
     def near(self):
-        self.wait((1, 0))
-        self.push((1, 0), (2, 0), self.along_first(True))
-        self.spread(1)
-        self.wait((3, 0))
-        self.spread(3)
+        came, other = (1, 3) if self.turn == 0 else (3, 1)
+        self.wait((came, 0))
+        self.push((came, 0), (2, 0), self.along_first(self.turn == 0))
+        self.spread(came)
+        self.wait((other, 0))
+        self.spread(other)
         self.relay(0)
 
     def far(self):
@@ -149,7 +153,8 @@
         self.relay(2)
 
     def arrive(self):
-        self.wait((0, 3), (1, 1), (3, 1), (2, 3), (0, 2), (1, 2), (3, 2), (2, 2))
+        for df in (0, 1, 3, 2):
+            self.wait((df, 3 if self.ahead(df) else 1), (df, 2))
 
     def finish(self):
         for copy in self.sent:
@@ -158,31 +163,39 @@
 
 class Exchange:
     def __init__(self, axis, size, me, block, send, recv):
-        self.axis, self.size, self.me, self.block = axis, size, me, block
-        self.send, self.recv = send, recv
+        inner = size // SIDE
+        self.axis, self.me, self.block = axis, me, block
+        self.send, self.recv, self.inner = send, recv, inner
+        self.outer_at, self.inner_at = lax.div(me, inner), lax.rem(me, inner)
+        steps = [(o, i) for o in range(SIDE) for i in range(inner) if (o, i) != (0, 0)]
+        self.steps = sorted(steps, key=lambda s: -(min(s[0], SIDE - s[0]) + min(s[1], inner - s[1])))
         self.sent = []
 
-    def copy(self, owner, step, to):
+    def device(self, outer, inner):
+        o = lax.rem(self.outer_at + SIDE + outer, SIDE)
+        return o * self.inner + lax.rem(self.inner_at + self.inner + inner, self.inner)
+
+    def copy(self, owner, place, to):
         ref = self.block(owner)
         return pltpu.make_async_remote_copy(
             src_ref=ref,
             dst_ref=ref,
-            send_sem=self.send.at[step],
-            recv_sem=self.recv.at[step],
+            send_sem=self.send.at[place],
+            recv_sem=self.recv.at[place],
             device_id={self.axis: to},
             device_id_type=MESH,
         )
 
     def start(self):
-        for step in range(1, self.size):
-            copy = self.copy(self.me, step, lax.rem(self.me + step, self.size))
+        for place, (outer, inner) in enumerate(self.steps):
+            copy = self.copy(self.me, place, self.device(outer, inner))
             copy.start()
             self.sent.append(copy)
 
     def wait(self):
-        for step in range(1, self.size):
-            owner = lax.rem(self.me + self.size - step, self.size)
-            self.copy(owner, step, owner).wait_recv()
+        for place, (outer, inner) in enumerate(self.steps):
+            owner = self.device(-outer, -inner)
+            self.copy(owner, place, owner).wait_recv()
 
     def finish(self):
         for copy in self.sent:
@@ -269,15 +282,24 @@
 
     pl.semaphore_wait(barrier, len(beside))
 
-    def gathers(slot_of, send, recv):
+    def gathers(slot_of, send, recv, turn=0):
         return [
-            Gather(half, me, lambda dev, half=half: slot_of(half, dev), send, recv)
+            Gather(half, me, lambda dev, half=half: slot_of(half, dev), send, recv, turn)
             for half in range(2)
         ]
 
-    block_gathers = gathers(
-        lambda half, dev: blocks.at[2 * dev + half], blocks_send, blocks_recv
-    )
+    block_gathers = [
+        gather
+        for part in range(2)
+        for gather in gathers(
+            lambda half, dev, part=part: blocks.at[
+                2 * dev + half, :, pl.ds(part * (LEAF // 2), LEAF // 2)
+            ],
+            blocks_send.at[part],
+            blocks_recv.at[part],
+            part,
+        )
+    ]
     small_gathers = gathers(lambda half, dev: smalls.at[half, dev], smalls_send, smalls_recv)
     image_gather = gathers(
         lambda half, dev: fields1.at[2 * dev + half], image0_send, image0_recv
@@ -569,8 +591,8 @@
             pltpu.VMEM((TARGETS, BLOCK), F32),
             pltpu.VMEM((KEPT, 2, LEAF, LEAF), BF16),
             dma((2,)),
-            dma((messages,)),
-            dma((messages,)),
+            dma((2, messages)),
+            dma((2, messages)),
             dma((messages,)),
             dma((messages,)),
             dma((messages,)),

time: 94.4 us -> 92.3 us (0.978)
  Pallas kernels: 91.3 us -> 89.2 us
    pallas_call x1, Pallas kernels: 91.3 us -> 89.2 us  [on_device(): pl.pallas_call(body, out_shape=(out,) * 5, in_specs=[vmem, vmem, smem, sm...]
where the time goes in v1:
time: 92.3 us; the launch traced here: 92.1 us
  Pallas kernels  89.2 us (97%)
  other arithmetic  1.63 us (2%)
  between operations  1.29 us (1%)
    pallas_call x1, Pallas kernels, on_device(): pl.pallas_call(body, out_shape=(out,) * 5, in_specs=[vmem, vmem, smem, sm...  89.2 us

profile of v1, /device:TPU:1, one launch (start us, length us, event | category | flops | bytes accessed | tf_op | source)
XLA Modules:
  0.0 92.1 jit_solution(221632808796765779)
XLA Ops:
  1.3 89.2 %shard_map.104 = (f32[8,2048]{1,0:T(8,128)}, f32[8,2048]{1,0:T(8,128)}, f32[8,2048]{1,0:T(8,128)}, f32[8,2048]{1,0:T(8,128)}, f32[8,2048]{1,0:T(8,128)}) custom-call(bf16[32,2048]{1,0:T(8,128)(2,1)} %points_ref.1, f32[8,2048]{1,0:T(8,128)} %right_ref.1, s32[2,8]{1,0:T(2,128)} %listed_ref.1, s32[2]{0:T(128)} %count_ref.1, s32[1,256]{1,0:T(1,128)} %mid_pick_ref.1, ...), custom_call_target="tpu_custom_call" | custom-call | tf_op jit(solution)/shard_map/pallas_call | solution.py:571
  90.5 1.6 %multiply_subtract_fusion = (f32[8,2048]{1,0:T(8,128)}, f32[8,2048]{1,0:T(8,128)}) fusion(f32[8,2048]{1,0:T(8,128)} %get-tuple-element.10, f32[8,2048]{1,0:T(8,128)} %get-tuple-element.8, f32[8,2048]{1,0:T(8,128)} %get-tuple-element.11, f32[8,2048]{1,0:T(8,128)} %get-tuple-element.7, f32[8,2048]{1,0:T(8,128)} %get-tuple-element.9), kind=kLoop, calls=%fused_computation | loop fusion | flops 65536 | bytes 458752 | tf_op jit(solution)/shard_map/sub | solution.py:617

commit v2 on v1

--- a/solution.py
+++ b/solution.py
@@ -159,6 +159,25 @@
     def finish(self):
         for copy in self.sent:
             copy.wait_send()
+
+
+class ShortGather(Gather):
+    def own(self):
+        self.push((0, 0), (2, 0), self.device(2, 0))
+        super().own()
+
+    def near(self):
+        self.wait((1, 0))
+        self.spread(1)
+        self.wait((3, 0))
+        self.spread(3)
+        self.wait((2, 0))
+        self.spread(2)
+        self.relay(0)
+
+    def far(self):
+        for df in (1, 3, 2):
+            self.relay(df)
 
 
 class Exchange:
@@ -282,9 +301,9 @@
 
     pl.semaphore_wait(barrier, len(beside))
 
-    def gathers(slot_of, send, recv, turn=0):
+    def gathers(slot_of, send, recv, turn=0, kind=Gather):
         return [
-            Gather(half, me, lambda dev, half=half: slot_of(half, dev), send, recv, turn)
+            kind(half, me, lambda dev, half=half: slot_of(half, dev), send, recv, turn)
             for half in range(2)
         ]
 
@@ -300,9 +319,11 @@
             part,
         )
     ]
-    small_gathers = gathers(lambda half, dev: smalls.at[half, dev], smalls_send, smalls_recv)
+    small_gathers = gathers(
+        lambda half, dev: smalls.at[half, dev], smalls_send, smalls_recv, kind=ShortGather
+    )
     image_gather = gathers(
-        lambda half, dev: fields1.at[2 * dev + half], image0_send, image0_recv
+        lambda half, dev: fields1.at[2 * dev + half], image0_send, image0_recv, kind=ShortGather
     )[:1]
     image_exchange = Exchange(
         "leaf", N_LEAF, me, lambda dev: fields1.at[2 * dev + 1], image1_send, image1_recv
@@ -447,7 +468,7 @@
         return noise * value[:, columns] + near(slot) + term[:, columns]
 
     near_listed(0, 0, 1, 3)
-    step(small_gathers, "last", "arrive")
+    step(small_gathers, "arrive")
     own_root, top = jnp.zeros((FEATURES, RANK), F32), jnp.zeros((2 * TARGETS, RANK), F32)
     for dev in range(N_LEAF):
         own_root = own_root + smalls[1, dev, 0:FEATURES, :].astype(F32)
@@ -470,12 +491,11 @@
 
     finish_image(0)
     step(image_gather, "own")
-    near_listed(0, 1, 1, 4)
+    near_listed(0, 1, 1, 5)
     step(image_gather, "near")
-    near_listed(0, 1, 4, 7)
+    near_listed(0, 1, 5, SLOTS)
+    finish_image(1)
     step(image_gather, "far")
-    near_listed(0, 1, 7, SLOTS)
-    finish_image(1)
     image_exchange.start()
 
     def summed(value):
@@ -493,7 +513,6 @@
     )
     weight_exchange.start()
     near_self(1, 0)
-    step(image_gather, "last")
     near_self(1, 1)
     step(image_gather, "arrive")
     image_exchange.wait()

time: 92.3 us -> 90.9 us (0.985)
  Pallas kernels: 89.2 us -> 87.7 us
    pallas_call x1, Pallas kernels: 89.2 us -> 87.7 us  [on_device(): pl.pallas_call(body, out_shape=(out,) * 5, in_specs=[vmem, vmem, smem, sm...]
where the time goes in v2:
time: 90.9 us; the launch traced here: 90.7 us
  Pallas kernels  87.7 us (96%)
  other arithmetic  1.63 us (2%)
  between operations  1.29 us (1%)
    pallas_call x1, Pallas kernels, on_device(): pl.pallas_call(body, out_shape=(out,) * 5, in_specs=[vmem, vmem, smem, sm...  87.7 us

profile of v2, /device:TPU:1, one launch (start us, length us, event | category | flops | bytes accessed | tf_op | source)
XLA Modules:
  0.0 90.7 jit_solution(4811172042622193655)
XLA Ops:
  1.3 87.7 %shard_map.104 = (f32[8,2048]{1,0:T(8,128)}, f32[8,2048]{1,0:T(8,128)}, f32[8,2048]{1,0:T(8,128)}, f32[8,2048]{1,0:T(8,128)}, f32[8,2048]{1,0:T(8,128)}) custom-call(bf16[32,2048]{1,0:T(8,128)(2,1)} %points_ref.1, f32[8,2048]{1,0:T(8,128)} %right_ref.1, s32[2,8]{1,0:T(2,128)} %listed_ref.1, s32[2]{0:T(128)} %count_ref.1, s32[1,256]{1,0:T(1,128)} %mid_pick_ref.1, ...), custom_call_target="tpu_custom_call" | custom-call | tf_op jit(solution)/shard_map/pallas_call | solution.py:590
  89.0 1.6 %multiply_subtract_fusion = (f32[8,2048]{1,0:T(8,128)}, f32[8,2048]{1,0:T(8,128)}) fusion(f32[8,2048]{1,0:T(8,128)} %get-tuple-element.10, f32[8,2048]{1,0:T(8,128)} %get-tuple-element.8, f32[8,2048]{1,0:T(8,128)} %get-tuple-element.11, f32[8,2048]{1,0:T(8,128)} %get-tuple-element.7, f32[8,2048]{1,0:T(8,128)} %get-tuple-element.9), kind=kLoop, calls=%fused_computation | loop fusion | flops 65536 | bytes 458752 | tf_op jit(solution)/shard_map/sub | solution.py:636

commit v3 on v2

--- a/solution.py
+++ b/solution.py
@@ -517,6 +517,7 @@
     step(image_gather, "arrive")
     image_exchange.wait()
     near_listed(1, 0)
+    near_listed(1, 1, 1, 3)
     weight_exchange.wait()
     sums = weights[0, 8:24]
     for dev in range(1, N_LEAF):
@@ -525,7 +526,7 @@
     tops[grp, 8:16] = sums[8:16]
     top_exchange.start()
     mid_part = mid_image(lambda dev: stacked(weights[dev, 0:8]))
-    near_listed(1, 1)
+    near_listed(1, 1, 3, SLOTS)
     top_exchange.wait()
     expand(mid_part, lambda g: stacked(tops[g, 0:8]))
 

time: 90.9 us -> 90.9 us (level)
  no operation moved by 1% of the time
where the time goes in v3:
time: 90.9 us; the launch traced here: 90.7 us
  Pallas kernels  87.7 us (96%)
  other arithmetic  1.63 us (2%)
  between operations  1.29 us (1%)
    pallas_call x1, Pallas kernels, on_device(): pl.pallas_call(body, out_shape=(out,) * 5, in_specs=[vmem, vmem, smem, sm...  87.7 us

profile of v3, /device:TPU:1, one launch (start us, length us, event | category | flops | bytes accessed | tf_op | source)
XLA Modules:
  0.0 90.7 jit_solution(8726902908111396463)
XLA Ops:
  1.3 87.7 %shard_map.104 = (f32[8,2048]{1,0:T(8,128)}, f32[8,2048]{1,0:T(8,128)}, f32[8,2048]{1,0:T(8,128)}, f32[8,2048]{1,0:T(8,128)}, f32[8,2048]{1,0:T(8,128)}) custom-call(bf16[32,2048]{1,0:T(8,128)(2,1)} %points_ref.1, f32[8,2048]{1,0:T(8,128)} %right_ref.1, s32[2,8]{1,0:T(2,128)} %listed_ref.1, s32[2]{0:T(128)} %count_ref.1, s32[1,256]{1,0:T(1,128)} %mid_pick_ref.1, ...), custom_call_target="tpu_custom_call" | custom-call | tf_op jit(solution)/shard_map/pallas_call | solution.py:591
  89.0 1.6 %multiply_subtract_fusion = (f32[8,2048]{1,0:T(8,128)}, f32[8,2048]{1,0:T(8,128)}) fusion(f32[8,2048]{1,0:T(8,128)} %get-tuple-element.10, f32[8,2048]{1,0:T(8,128)} %get-tuple-element.8, f32[8,2048]{1,0:T(8,128)} %get-tuple-element.11, f32[8,2048]{1,0:T(8,128)} %get-tuple-element.7, f32[8,2048]{1,0:T(8,128)} %get-tuple-element.9), kind=kLoop, calls=%fused_computation | loop fusion | flops 65536 | bytes 458752 | tf_op jit(solution)/shard_map/sub | solution.py:637
